TPU v7x, 32 devices: a whole 2x2x4 slice. The times are simulated.
32 devices in a mesh: dp: 8 (over z, core), fsdp: 4 (over y, x).
Axes of the slice: x: 2, y: 2, z: 4, core: 2. Of those that a mesh axis runs over, the one named last changes fastest.
Arguments:
- tokens: bfloat16 [16384, 1024], P(('dp', 'fsdp')), may hold values from -6 to 6
- first_values: bfloat16 [16384, 1024], P(('dp', 'fsdp')), may hold values from -12 to 12
- lengths: int32 [32], P(('dp', 'fsdp')), may hold values from 256 to 512, as said below
- gain_one: bfloat16 [1024], P('fsdp'), may hold values from 0.099609375 to 1.8984375
- w_qkv: bfloat16 [1024, 3072], P('fsdp'), may hold values from -0.1875 to 0.1875
- w_out: bfloat16 [1024, 1024], P('fsdp'), may hold values from -3 to 3
- gain_two: bfloat16 [1024], P('fsdp'), may hold values from 0.099609375 to 1.8984375
- w_gate: bfloat16 [1024, 2816], P('fsdp'), may hold values from -0.1875 to 0.1875
- w_up: bfloat16 [1024, 2816], P('fsdp'), may hold values from -0.1875 to 0.1875
- w_down: bfloat16 [2816, 1024], P('fsdp'), may hold values from -0.4375 to 0.4375
- cotangent: bfloat16 [16384, 1024], P(('dp', 'fsdp')), may hold values from -6 to 6
Outputs:
- output: bfloat16 [16384, 1024], P(('dp', 'fsdp'))
- grad_tokens: float32 [16384, 1024], P(('dp', 'fsdp'))
- grad_first_values: float32 [16384, 1024], P(('dp', 'fsdp'))
- grad_gain_one: float32 [1024], P('fsdp')
- grad_w_qkv: float32 [1024, 3072], P('fsdp')
- grad_w_out: float32 [1024, 1024], P('fsdp')
- grad_gain_two: float32 [1024], P('fsdp')
- grad_w_gate: float32 [1024, 2816], P('fsdp')
- grad_w_up: float32 [1024, 2816], P('fsdp')
- grad_w_down: float32 [2816, 1024], P('fsdp')
- first_norm: float32 [], replicated
- value_norm: float32 [], replicated
Inputs may be any that keep to these rules, and one draw needn't show every extreme that they name: `lengths`: each device holds one whole sequence in its 512 rows; rows from its length on are padding that no query reads.
All inputs are finite; a program needn't handle non-finite values.
Results may differ from a plain program's by a relative error of at most 0.015.
Values may be sent and summed in bfloat16 or wider, within the bound.
A program may use at most 192 MiB of HBM per device.

v0:
```python
import functools
import math

import jax
import jax.numpy as jnp
import numpy as np
from jax import lax
from jax.experimental import pallas as pl
from jax.experimental.pallas import tpu as pltpu
from jax.sharding import PartitionSpec as P

HEAD_DIM = 64
PAIR = 2 * HEAD_DIM
TILE = 256
GAIN_ROWS = 16
norm_eps = 1e-06
F32 = jnp.float32
BF16 = jnp.bfloat16
AXES = ("dp", "fsdp")
ANY = pl.BlockSpec(memory_space=pl.ANY)


def dot_nn(a, b):
    return lax.dot_general(a, b, (((1,), (0,)), ((), ())), preferred_element_type=F32)


def dot_nt(a, b):
    return lax.dot_general(a, b, (((1,), (1,)), ((), ())), preferred_element_type=F32)


def dot_tn(a, b):
    return lax.dot_general(a, b, (((0,), (0,)), ((), ())), preferred_element_type=F32)


def rotary_tables(count):
    half = HEAD_DIM // 2
    frequency = np.exp(
        -(np.arange(half, dtype=np.float32) * np.float32(2.0) / np.float32(HEAD_DIM))
        * np.float32(math.log(10000.0))
    ).astype(np.float32)
    angles = np.arange(count, dtype=np.float32)[:, None] * frequency[None, :]
    cosine = np.cos(angles.astype(np.float64)).astype(np.float32)
    sine = np.sin(angles.astype(np.float64)).astype(np.float32)
    cosine = np.concatenate([cosine] * 4, axis=1)
    sine = np.concatenate([-sine, sine, -sine, sine], axis=1)
    return cosine, sine


def swap_halves(x):
    half = HEAD_DIM // 2
    lane = lax.broadcasted_iota(jnp.int32, x.shape, 1)
    up = pltpu.roll(x, PAIR - half, 1)
    down = pltpu.roll(x, half, 1)
    return jnp.where((lane % HEAD_DIM) < half, up, down)


class Layout:
    def __init__(self, dp, fs):
        self.dp, self.fs = dp, fs
        self.bits = fs.bit_length() - 1
        self.line = dp // 2


def add_low(a, b):
    return (a.astype(F32) + b.astype(F32)).astype(BF16)


def start(copies):
    for copy in copies:
        copy.start()


def wait(copies):
    for copy in copies:
        copy.wait()


def struct(shape, dtype):
    return jax.ShapeDtypeStruct(shape, dtype)


class Place:
    def __init__(self, lay):
        self.bits, self.count = lay.bits, lay.fs
        self.d, self.f = lax.axis_index("dp"), lax.axis_index("fsdp")
        self.c = lax.rem(self.d, 2)
        self.flips = []
        for i in range(self.bits):
            ahead, back = 1 << i, 1 << (self.bits - 1 - i)
            one = ahead * (1 - 2 * lax.rem(self.f // ahead, 2))
            two = back * (1 - 2 * lax.rem(self.f // back, 2))
            self.flips.append(one + self.c * (two - one))

    def shard(self, m):
        return self.f + sum(self.flips[i] for i in range(self.bits) if (m >> i) & 1)

    def partner(self, i):
        return (self.d, self.f + self.flips[i])

    def sibling(self):
        return (self.d + 1 - 2 * self.c, self.f)

    def above(self):
        return (self.d + 2 - 4 * lax.rem(self.d // 2, 2), self.f)

    def group(self):
        others = []
        for m in range(1, self.count):
            others.append((self.d, self.shard(m)))
        return others


def remote(src, dst, send, recv, device):
    return pltpu.make_async_remote_copy(
        src_ref=src,
        dst_ref=dst,
        send_sem=send,
        recv_sem=recv,
        device_id=device,
        device_id_type=pl.DeviceIdType.MESH,
    )


class Gather:
    def __init__(self, place, own, full, first, total, lifted, sems, slot):
        self.place = place
        send, recv, up_send, up_recv, cross_send, cross_recv, more_send, more_recv = sems
        count = place.count
        rows, side = own.shape[0], total // 2
        column = pl.ds(pl.multiple_of(first + place.c * side, 128), side)
        size = rows // 2 if lifted else rows
        parity = lax.rem(place.d // 2, 2) if lifted else 0
        self.link, self.up, self.cross, self.more = [None], [None], [None], [None]

        def spot(piece, which):
            at = pl.multiple_of(place.shard(piece) * rows + which * size, size)
            return full.at[pl.ds(at, size), column]

        for m in range(1, count):
            step = m.bit_length() - 1
            before = m - (1 << step)
            source = spot(before, parity)
            if before == 0:
                source = own.at[pl.ds(pl.multiple_of(parity * size, size), size), column]
            at = slot * count + m
            self.link.append(
                remote(source, spot(before, parity), send.at[at], recv.at[at], place.partner(step))
            )
            here = spot(m, parity)
            self.cross.append(
                remote(here, here, cross_send.at[at], cross_recv.at[at], place.sibling())
            )
            if lifted:
                there = spot(m, 1 - parity)
                self.up.append(remote(here, here, up_send.at[at], up_recv.at[at], place.above()))
                self.more.append(
                    remote(there, there, more_send.at[at], more_recv.at[at], place.sibling())
                )

    def begin(self, m):
        self.link[m].start()

    def arrived(self, m):
        self.link[m].wait_recv()
        for i in range(m.bit_length(), self.place.bits):
            self.link[m + (1 << i)].start()
        self.cross[m].start()

    def lift(self, m):
        self.up[m].start()

    def landed(self, m):
        self.up[m].wait_recv()
        self.more[m].start()

    def complete(self):
        for copy in self.cross[1:] + self.more[1:]:
            copy.wait_recv()

    def drain(self):
        for copy in self.link[1:] + self.cross[1:] + self.up[1:] + self.more[1:]:
            copy.wait_send()


QK, V, OUT, GATE, UP, DOWN = range(6)
BEGIN, ARRIVE, LIFT, LAND = range(4)
NORMALISE, QUERIES, KEYS, VALUES, HEADS, PROJECT, GATES, UPS, SUM_DOWN = range(4, 13)
FORWARD_LIFTED = (QK, V, GATE, DOWN)
FORWARD_ORDER = (
    (BEGIN, QK, 1), (BEGIN, QK, 2), (BEGIN, V, 1), (BEGIN, V, 2), (BEGIN, GATE, 1),
    (NORMALISE, 0, 0), (ARRIVE, QK, 1), (ARRIVE, QK, 2), (LIFT, QK, 1), (LIFT, QK, 2),
    (ARRIVE, V, 1), (BEGIN, GATE, 2), (ARRIVE, V, 2), (ARRIVE, GATE, 1), (BEGIN, OUT, 1),
    (ARRIVE, QK, 3), (LIFT, QK, 3), (LAND, QK, 1), (LIFT, V, 1), (BEGIN, UP, 1), (ARRIVE, V, 3),
    (BEGIN, OUT, 2), (LIFT, V, 2), (LAND, QK, 2), (ARRIVE, OUT, 1), (BEGIN, DOWN, 1), (LIFT, V, 3),
    (LAND, QK, 3), (QUERIES, 0, 0), (ARRIVE, GATE, 2), (LAND, V, 1), (KEYS, 0, 0), (LIFT, GATE, 1),
    (LAND, V, 2), (LIFT, GATE, 2), (ARRIVE, OUT, 2), (LAND, V, 3), (VALUES, 0, 0), (BEGIN, UP, 2),
    (HEADS, 0, 0), (ARRIVE, UP, 1), (ARRIVE, GATE, 3), (HEADS, 0, 0), (LAND, GATE, 1),
    (LIFT, GATE, 3), (ARRIVE, OUT, 3), (BEGIN, DOWN, 2), (HEADS, 0, 0), (ARRIVE, DOWN, 1),
    (LAND, GATE, 2), (HEADS, 0, 0), (LIFT, DOWN, 1), (PROJECT, 0, 0), (LAND, GATE, 3),
    (ARRIVE, UP, 2), (GATES, 0, 0), (ARRIVE, UP, 3), (ARRIVE, DOWN, 2), (LIFT, DOWN, 2),
    (UPS, 0, 0), (ARRIVE, DOWN, 3), (LIFT, DOWN, 3), (LAND, DOWN, 1), (UPS, 0, 1), (LAND, DOWN, 2),
    (SUM_DOWN, 0, 0), (LAND, DOWN, 3),
)


def forward_body(
    lay,
    lengths,
    in_tokens,
    in_first,
    in_cosine,
    in_sine,
    gain_one_in,
    gain_two_in,
    cotangent,
    in_qkv,
    in_out,
    in_gate,
    in_up,
    in_down,
    full_qkv,
    full_out,
    full_gate,
    full_up,
    full_down,
    out_q,
    out_k,
    out_v,
    logs,
    hidden_one2,
    attended2,
    hidden_two2,
    out_after,
    out_gate,
    out_up,
    out_product,
    grad_down,
    gains,
    sums,
    w_qkv,
    w_out,
    w_gate,
    w_up,
    tokens,
    first,
    cosine,
    sine,
    gain_in,
    gain,
    hidden,
    queries,
    keys,
    values,
    attended,
    after,
    gate_pre,
    low_gate,
    low_up,
    product2,
    cot2,
    grad_low,
    turned,
    send,
    recv,
    up_send,
    up_recv,
    cross_send,
    cross_recv,
    more_send,
    more_recv,
    local,
    gain_send,
    gain_recv,
    swap_send,
    swap_recv,
    write,
):
    place = Place(lay)
    count, c = place.count, place.c
    rows, width = tokens.shape
    shard_rows = in_qkv.shape[0]
    ff = in_gate.shape[1]
    sibling = place.sibling()

    barrier = pltpu.get_barrier_semaphore()
    begins = []
    for i, (source, target) in enumerate(
        ((in_tokens, tokens), (in_cosine, cosine), (in_sine, sine), (in_first, first))
    ):
        begins.append(pltpu.make_async_copy(source, target, local.at[10 + i]))
    start(begins)
    known = [sibling, place.above()] + place.group()
    for device in known:
        pl.semaphore_signal(barrier, inc=1, device_id=device, device_id_type=pl.DeviceIdType.MESH)
    pl.semaphore_wait(barrier, len(known))

    sems = (send, recv, up_send, up_recv, cross_send, cross_recv, more_send, more_recv)

    def gather(who, own, full, first_column, total):
        return Gather(place, own, full, first_column, total, who in FORWARD_LIFTED, sems, who)

    gathers = {
        QK: gather(QK, in_qkv, w_qkv, 0, 2 * width),
        V: gather(V, in_qkv, w_qkv, 2 * width, width),
        OUT: gather(OUT, in_out, w_out, 0, width),
        GATE: gather(GATE, in_gate, w_gate, 0, ff),
        UP: gather(UP, in_up, w_up, 0, ff),
        DOWN: gather(DOWN, in_down, full_down, 0, width),
    }

    seen = {}

    def link(step):
        kind, who, turn = step
        one = gathers[who]
        if kind == BEGIN:
            firsts = [1 << i for i in range(place.bits)]
            for m in firsts[turn - 1 : turn] if count == 4 else firsts * (turn == 1):
                one.begin(m)
            return
        if count == 4:
            pieces = [turn]
        else:
            done = seen[who, kind] = seen.get((who, kind), 0) + 1
            pieces = range(1 + (done - 1) * (count - 1) // 3, 1 + done * (count - 1) // 3)
        for m in pieces:
            {ARRIVE: one.arrived, LIFT: one.lift, LAND: one.landed}[kind](m)

    gain_in[...] = jnp.zeros(gain_in.shape, BF16)
    gain_in[0:1, :] = gain_one_in[...].reshape(1, shard_rows)
    gain_in[1:2, :] = gain_two_in[...].reshape(1, shard_rows)
    gain_at = pl.multiple_of(place.f * shard_rows, shard_rows)
    gain_copies = []
    for m, device in enumerate(place.group()):
        gain_copies.append(
            remote(
                gain_in,
                gain.at[:, pl.ds(gain_at, shard_rows)],
                gain_send.at[m],
                gain_recv.at[m],
                device,
            )
        )
    gain_own = pltpu.make_async_copy(
        gain_in, gain.at[:, pl.ds(gain_at, shard_rows)], local.at[4]
    )
    start(gain_copies + [gain_own])
    order = list(FORWARD_ORDER)
    while order[0][0] == BEGIN:
        link(order.pop(0))
    own_rows = pl.ds(gain_at, shard_rows)
    locals_of = {}
    for slot, (name, source, full) in enumerate(
        ((QK, in_qkv, w_qkv), (OUT, in_out, w_out), (GATE, in_gate, w_gate), (UP, in_up, w_up))
    ):
        locals_of[name] = pltpu.make_async_copy(source, full.at[own_rows, :], local.at[slot])
        locals_of[name].start()
    half = width // 2
    down_rows = in_down.shape[0]
    down_at = pl.ds(pl.multiple_of(place.f * down_rows, down_rows), down_rows)
    down_in, down_out = [], []
    for i in range(2):
        stage = grad_low.at[pl.ds(i * down_rows, down_rows), :]
        side = pl.ds(i * half, half)
        down_in.append(pltpu.make_async_copy(in_down.at[:, side], stage, local.at[6 + i]))
        down_out.append(pltpu.make_async_copy(stage, full_down.at[down_at, side], local.at[8 + i]))
    start(down_in)

    writes = []

    def put(source, target):
        copy = pltpu.make_async_copy(source, target, write.at[len(writes)])
        copy.start()
        writes.append(copy)

    swaps = []

    def swap(source, target):
        slot = len(swaps)
        copy = remote(source, target, swap_send.at[slot], swap_recv.at[slot], sibling)
        copy.start()
        swaps.append(copy)
        return copy

    def share(source, target):
        put(source, target.at[pl.ds(0, rows), :])
        return swap(source, target.at[pl.ds(rows, rows), :])

    theirs = pl.multiple_of((1 - c) * half, 128)
    ours = pl.multiple_of(c * half, 128)
    cot_swap = swap(cotangent.at[:, pl.ds(theirs, half)], cot2.at[pl.ds(rows, rows), :])
    cot_own = pltpu.make_async_copy(
        cotangent.at[:, pl.ds(ours, half)], cot2.at[pl.ds(0, rows), :], local.at[5]
    )
    cot_own.start()

    block = min(TILE, rows)
    length = lengths[0]
    pairs = width // PAIR
    hidden_two = low_up.at[:, pl.ds(0, width)]
    two_swap, two_put, product_swaps = [], [], []

    def by_rows(step):
        @pl.loop(0, rows // block)
        def _(i):
            step(pl.ds(pl.multiple_of(i * block, block), block))

    def normalise():
        begins[0].wait()
        inputs = tokens[...].astype(F32)
        inverse = lax.rsqrt(jnp.mean(inputs * inputs, axis=-1, keepdims=True) + norm_eps)
        for copy in gain_copies:
            copy.wait_recv()
        gain_own.wait()
        gains[0:1, :] = gain[0:1, :].astype(F32)
        gains[1:2, :] = gain[1:2, :].astype(F32)
        gains[2:8, :] = jnp.zeros((6, width), F32)
        hidden[...] = (inputs * inverse * gains[0:1, :]).astype(BF16)
        share(hidden, hidden_one2)
        wait(down_in)
        start(down_out)
        sums[...] = jnp.zeros(sums.shape, F32)
        logs[...] = jnp.zeros(logs.shape, F32)

    def rotated(which, out, scale):
        def step(at):
            cos, sin = cosine[at, :], sine[at, :]
            raw = dot_nn(hidden[at, :], w_qkv[:, which * width : (which + 1) * width])
            for p in range(width // PAIR):
                x = raw[:, p * PAIR : (p + 1) * PAIR]
                low = (x * cos + swap_halves(x) * sin).astype(BF16)
                out[at, p * PAIR : (p + 1) * PAIR] = low * jnp.asarray(scale, BF16)

        by_rows(step)

    def mix(at):
        raw = dot_nn(hidden[at, :], w_qkv[:, 2 * width : 3 * width])
        kept = first[at, :].astype(F32)
        mixed = 0.5 * raw + 0.5 * kept
        values[at, :] = mixed.astype(BF16)
        sums[0:1, :] += jnp.sum(kept * kept, axis=0, keepdims=True)
        sums[1:2, :] += jnp.sum(mixed * mixed, axis=0, keepdims=True)

    turn = 2

    def attend(links):
        @pl.loop(0, pairs // turn)
        def _(i):
            for j in range(turn):
                attend_pair(i * turn + j, turned.at[j])
            for after_turn, steps in enumerate(links):
                if steps:

                    @pl.when(i == after_turn)
                    def _():
                        for step in steps:
                            link(step)

    def attend_pair(p, turned):
        at = pl.ds(pl.multiple_of(p * PAIR, PAIR), PAIR)
        q, k = queries[:, at], keys[:, at]
        v_t = values[:, at].T
        lane = lax.broadcasted_iota(jnp.int32, (rows, PAIR), 1)
        for head in range(2):
            inside = (lane // HEAD_DIM) == head
            k_head = jnp.where(inside, k, jnp.zeros_like(k))
            v_head = v_t[head * HEAD_DIM : (head + 1) * HEAD_DIM]
            for b in range(rows // block):
                upto = (b + 1) * block
                scores = dot_nt(k_head[:upto], q[b * block : upto])
                key = lax.broadcasted_iota(jnp.int32, scores.shape, 0)
                query = lax.broadcasted_iota(jnp.int32, (1, block), 1) + b * block
                allowed = key <= jnp.minimum(query, length - 1)
                scores = jnp.where(allowed, scores, -1e30)
                peak = jnp.max(scores, axis=0, keepdims=True)
                expo = jnp.exp(scores - peak)
                total = jnp.sum(expo, axis=0, keepdims=True)
                logs[p, head : head + 1, b * block : upto] = peak + jnp.log(total)
                out = dot_nn(v_head[:, :upto], expo.astype(BF16)) * (1.0 / total)
                turned[head * HEAD_DIM : (head + 1) * HEAD_DIM, b * block : upto] = out
        attended[:, at] = turned[...].T.astype(BF16)

    def project(at):
        x = tokens[at, :].astype(F32) + dot_nn(attended[at, :], w_out[...])
        after[at, :] = x
        scale = lax.rsqrt(jnp.mean(x * x, axis=-1, keepdims=True) + norm_eps)
        low_up[at, 0:width] = (x * scale * gains[1:2, :]).astype(BF16)

    def gate_rows(at):
        gate_pre[at, :] = dot_nn(low_up[at, 0:width], w_gate[...])
        low_gate[at, :] = gate_pre[at, :].astype(BF16)

    def up_rows(at):
        up_proj = dot_nn(low_up[at, 0:width], w_up[...])
        gate_of = gate_pre[at, :]
        product2[at, :] = (gate_of * jax.nn.sigmoid(gate_of) * up_proj).astype(BF16)
        low_up[at, :] = up_proj.astype(BF16)

    def compute(kind, part):
        if kind == NORMALISE:
            normalise()
        elif kind == QUERIES:
            wait(begins[1:])
            locals_of[QK].wait()
            gathers[QK].complete()
            rotated(0, queries, HEAD_DIM**-0.5)
            put(queries, out_q)
        elif kind == KEYS:
            rotated(1, keys, 1.0)
            put(keys, out_k)
        elif kind == VALUES:
            gathers[V].complete()
            put(w_qkv, full_qkv)
            by_rows(mix)
            put(values, out_v)
        elif kind == PROJECT:
            share(attended, attended2)
            locals_of[OUT].wait()
            gathers[OUT].complete()
            put(w_out, full_out)
            by_rows(project)
            put(after, out_after)
            two_swap.append(share(hidden_two, hidden_two2))
            two_put.append(writes[-1])
        elif kind == GATES:
            locals_of[GATE].wait()
            gathers[GATE].complete()
            put(w_gate, full_gate)
            by_rows(gate_rows)
            put(low_gate, out_gate)
        elif kind == UPS and part == 0:
            locals_of[UP].wait()
            gathers[UP].complete()
            put(w_up, full_up)
            two_swap[0].wait_send()
            two_put[0].wait()
            steps = []
            while order[0][0] <= LAND:
                steps.append(order.pop(0))
            up_parts(steps)
        elif kind == UPS:
            put(low_up, out_up)
            put(product2.at[pl.ds(0, rows), :], out_product)
        else:
            wait(down_out)
            cot_own.wait()
            cot_swap.wait_recv()
            for copy in product_swaps:
                copy.wait_recv()

            @pl.loop(0, ff // TILE)
            def _(i):
                at = pl.ds(pl.multiple_of(i * TILE, TILE), TILE)
                grad_low[at, :] = dot_tn(product2[:, at], cot2[...]).astype(BF16)

            put(grad_low, grad_down)

    def up_parts(steps):
        size = rows // 2
        for i in range(2):
            part = pl.ds(i * size, size)
            there = pl.ds(rows + i * size, size)
            slot = len(swaps)
            copy = remote(
                product2.at[part, :], product2.at[there, :], swap_send.at[slot], swap_recv.at[slot], sibling
            )
            swaps.append(copy)
            product_swaps.append(copy)

        @pl.loop(0, 2)
        def _(i):
            up_rows(pl.ds(pl.multiple_of(i * size, size), size))

            @pl.when(i == 0)
            def _():
                product_swaps[0].start()
                for step in steps:
                    link(step)

            @pl.when(i == 1)
            def _():
                product_swaps[1].start()

    while order:
        step = order.pop(0)
        if step[0] <= LAND:
            link(step)
        elif step[0] == HEADS:
            turns = pairs // turn
            links, at = [[] for _ in range(4)], 0
            while order and (order[0][0] <= LAND or order[0][0] == HEADS):
                if order[0][0] == HEADS:
                    order.pop(0)
                    at += 1
                else:
                    links[at].append(order.pop(0))
            spread = [[] for _ in range(turns)]
            for i, steps in enumerate(links):
                spread[(i + 1) * turns // 4 - 1] += steps
            attend(spread)
        else:
            compute(step[0], step[2])

    gathers[DOWN].complete()
    for one in gathers.values():
        one.drain()
    for copy in gain_copies:
        copy.wait_send()
    waited = [cot_swap, *product_swaps]
    for copy in swaps:
        if not any(copy is item for item in waited):
            copy.wait_recv()
        if copy is not two_swap[0]:
            copy.wait_send()
    for copy in writes:
        if copy is not two_put[0]:
            copy.wait()


def forward_kernel(lay, lengths, tokens, first, tables, gain_one, gain_two, cotangent, w_qkv, w_out, w_gate, w_up, w_down):
    count = lay.fs
    rows, width = tokens.shape
    n, ff = w_qkv.shape[1], w_gate.shape[1]
    half = width // 2
    pairs = width // PAIR
    big = struct((rows, width), BF16)
    wide = struct((rows, ff), BF16)
    two = struct((2 * rows, width), BF16)
    dma = pltpu.SemaphoreType.DMA
    vmem = pl.BlockSpec(memory_space=pltpu.VMEM)
    weights = [(width, n), (width, width), (width, ff), (width, ff), (ff, width)]
    out_shape = (
        [struct(shape, BF16) for shape in weights]
        + [big, big, big, struct((pairs, 8, rows), F32)]
        + [two, two, two, struct((rows, width), F32), wide, wide, wide]
        + [struct((ff, half), BF16), struct((8, width), F32), struct((8, width), F32)]
    )
    out_specs = [ANY] * 8 + [vmem] + [ANY] * 8 + [vmem, vmem]
    return pl.pallas_call(
        functools.partial(forward_body, lay),
        in_specs=[pl.BlockSpec(memory_space=pltpu.SMEM)] + [ANY] * 4 + [vmem] * 2 + [ANY] * 6,
        out_specs=out_specs,
        out_shape=out_shape,
        scratch_shapes=[
            pltpu.VMEM((width, n), BF16),
            pltpu.VMEM((width, width), BF16),
            pltpu.VMEM((width, ff), BF16),
            pltpu.VMEM((width, ff), BF16),
            pltpu.VMEM((rows, width), BF16),
            pltpu.VMEM((rows, width), BF16),
            pltpu.VMEM((rows, PAIR), F32),
            pltpu.VMEM((rows, PAIR), F32),
            pltpu.VMEM((GAIN_ROWS, width // count), BF16),
            pltpu.VMEM((GAIN_ROWS, width), BF16),
            pltpu.VMEM((rows, width), BF16),
            pltpu.VMEM((rows, width), BF16),
            pltpu.VMEM((rows, width), BF16),
            pltpu.VMEM((rows, width), BF16),
            pltpu.VMEM((rows, width), BF16),
            pltpu.VMEM((rows, width), F32),
            pltpu.VMEM((rows, ff), F32),
            pltpu.VMEM((rows, ff), BF16),
            pltpu.VMEM((rows, ff), BF16),
            pltpu.VMEM((2 * rows, ff), BF16),
            pltpu.VMEM((2 * rows, half), BF16),
            pltpu.VMEM((ff, half), BF16),
            pltpu.VMEM((2, PAIR, rows), F32),
            *[dma((6 * count,))] * 8,
            dma((14,)),
            dma((count - 1,)),
            dma((count - 1,)),
            dma((6,)),
            dma((6,)),
            dma((16,)),
        ],
        compiler_params=pltpu.CompilerParams(
            collective_id=0, has_side_effects=True, vmem_limit_bytes=62 * 2**20
        ),
        cost_estimate=pl.CostEstimate(
            flops=2 * rows * width * (n + width + 3 * ff),
            bytes_accessed=60 * 2**20,
            transcendentals=0,
        ),
        name="forward",
    )(lengths, tokens, first, *tables, gain_one, gain_two, cotangent, w_qkv, w_out, w_gate, w_up, w_down)


def rms_back(grad, normed, inverse):
    return inverse * (grad - normed * jnp.mean(grad * normed, axis=-1, keepdims=True))


class Line:
    def __init__(self, lay, place):
        size = lay.line
        r = place.d // 2
        self.half = size // 2
        upper = r // self.half
        toward = 1 - 2 * upper
        self.depth = r * toward + upper * (size - 1)
        self.next = (place.d + 2 * toward, place.f)
        self.prev = (place.d - 2 * toward, place.f)
        self.middle = self.depth == self.half - 1
        self.inner = self.depth > 0
        self.others = []
        reach = 1
        while reach < size:
            self.others.append((place.d + 2 * reach * (1 - 2 * lax.rem(r // reach, 2)), place.f))
            reach *= 2


def signal(sem, device):
    pl.semaphore_signal(sem, inc=1, device_id=device, device_id_type=pl.DeviceIdType.MESH)


class Reduce:
    def __init__(
        self, place, line, slot, window, held, sources, first, later, final, column, sems
    ):
        send, recv, z_send, z_recv, credit, f_local, f_send, f_recv = sems
        self.place, self.line, self.held, self.window = place, line, held, window
        self.bits, count = place.bits, place.count
        self.count = count
        base = slot * count
        half = count // 2
        self.steps, self.lands = [], []
        at = 0
        for i in range(self.bits):
            blocks = count >> (i + 1)
            copies, lands = [], []
            for q in range(blocks):
                source = sources[q] if i == 0 else held.at[blocks + q, window]
                land = first.at[q, window] if i == 0 else later.at[at + q, window]
                index = base + q if i == 0 else base + half + at + q
                lands.append(land)
                copies.append(remote(source, land, send.at[index], recv.at[index], place.partner(i)))
            if i > 0:
                at += blocks
            self.steps.append(copies)
            self.lands.append(lands)
        mine, inner, outer = held.at[0, window], first.at[0, window], first.at[1, window]
        two = 2 * slot
        self.hops = {
            "in": remote(mine, inner, z_send.at[two], z_recv.at[two], line.next),
            "middle": remote(mine, outer, z_send.at[two], z_recv.at[two + 1], line.next),
            "back": remote(inner, outer, z_send.at[two + 1], z_recv.at[two + 1], line.prev),
            "out": remote(outer, outer, z_send.at[two + 1], z_recv.at[two + 1], line.prev),
        }
        self.mine, self.inner, self.outer = mine, inner, outer
        spot = final.at[window, column]
        self.ends = []
        for source in (inner, outer):
            self.ends.append(
                (
                    pltpu.make_async_copy(source, spot, f_local.at[slot]),
                    remote(source, spot, f_send.at[slot], f_recv.at[slot], place.sibling()),
                )
            )
        self.from_next, self.from_prev = credit.at[two], credit.at[two + 1]

    def begin(self, q):
        self.steps[0][q].start()

    def block(self, i, q):
        blocks = self.count >> (i + 1)
        self.steps[i][q].wait_recv()
        here = self.held.at[q, self.window]
        here[...] = add_low(here[...], self.lands[i][q][...])
        if i + 1 < self.bits and q >= blocks // 2:
            self.steps[i + 1][q - blocks // 2].start()

    def leaving(self):
        half = self.count // 2
        for q in reversed(range(half // 2, half)):
            self.block(0, q)

    def staying(self):
        for q in reversed(range(self.count // 4)):
            self.block(0, q)
        line = self.line

        @pl.when(line.middle)
        def _():
            signal(self.from_next, line.next)

        @pl.when(jnp.logical_not(line.middle))
        def _():
            signal(self.from_prev, line.next)

        @pl.when(line.inner)
        def _():
            signal(self.from_next, line.prev)

    def rest(self):
        for i in range(1, self.bits):
            for q in reversed(range(self.count >> (i + 1))):
                self.block(i, q)

        @pl.when(jnp.logical_not(self.line.inner))
        def _():
            self.onward()

    def onward(self):
        line = self.line
        pl.semaphore_wait(self.from_next, 1)

        @pl.when(line.middle)
        def _():
            self.hops["middle"].start()

        @pl.when(jnp.logical_not(line.middle))
        def _():
            self.hops["in"].start()

    def inward(self):
        @pl.when(self.line.inner)
        def _():
            self.hops["in"].wait_recv()
            self.mine[...] = add_low(self.mine[...], self.inner[...])
            self.onward()

    def finish(self, which):
        local, cross = self.ends[which]
        local.start()
        cross.start()

    def across(self):
        line = self.line

        @pl.when(line.middle)
        def _():
            self.hops["middle"].wait_recv()
            self.inner[...] = add_low(self.mine[...], self.outer[...])

            @pl.when(line.inner)
            def _():
                pl.semaphore_wait(self.from_prev, 1)
                self.hops["back"].start()

            self.finish(0)

    def outward(self):
        line = self.line
        if line.half == 1:
            return

        @pl.when(jnp.logical_not(line.middle))
        def _():
            self.hops["out"].wait_recv()

            @pl.when(line.inner)
            def _():
                pl.semaphore_wait(self.from_prev, 1)
                self.hops["out"].start()

            self.finish(1)

    def drain(self):
        for copies in self.steps:
            for copy in copies:
                copy.wait_send()
        self.hops["in"].wait_send()

        @pl.when(self.line.inner)
        def _():
            self.hops["out"].wait_send()

        local, cross = self.ends[0]
        local.wait()
        cross.wait_send()
        cross.wait_recv()


W_DOWN, W_GATE, W_UP, W_OUT, W_V, W_K, W_Q = range(7)
BACKWARD_PARTS = (2, 2, 4, 2, 2, 2, 2)
LEAVING, STAYING, REST, INWARD, ACROSS, OUTWARD, SMALL = range(7)
BLOCKS, MLP_TILES, NORM_TWO, ATTEND_GRAD, HEAD_PAIRS, QKV_TILES, NORM_ONE = range(7, 14)
BACKWARD_ORDER = (
    (LEAVING, W_DOWN, 0), (STAYING, W_DOWN, 0), (BLOCKS, W_GATE, 3), (BLOCKS, W_GATE, 2),
    (LEAVING, W_DOWN, 1), (BLOCKS, W_GATE, 1), (REST, W_DOWN, 0), (BLOCKS, W_GATE, 0),
    (BLOCKS, W_UP, 3), (BLOCKS, W_UP, 2), (BLOCKS, W_UP, 1), (BLOCKS, W_UP, 0),
    (STAYING, W_DOWN, 1), (MLP_TILES, 0, 0), (REST, W_DOWN, 1), (INWARD, W_DOWN, 0),
    (LEAVING, W_GATE, 0), (MLP_TILES, 0, 1), (MLP_TILES, 0, 2), (MLP_TILES, 0, 3),
    (LEAVING, W_GATE, 1), (NORM_TWO, 0, 0), (INWARD, W_DOWN, 1), (ACROSS, W_DOWN, 0),
    (ATTEND_GRAD, 0, 0), (STAYING, W_GATE, 0), (REST, W_GATE, 0), (BLOCKS, W_OUT, 3),
    (BLOCKS, W_OUT, 2), (BLOCKS, W_OUT, 1), (BLOCKS, W_OUT, 0), (HEAD_PAIRS, 0, 0),
    (STAYING, W_GATE, 1), (REST, W_GATE, 1), (HEAD_PAIRS, 0, 1), (LEAVING, W_UP, 0),
    (LEAVING, W_UP, 1), (INWARD, W_GATE, 0), (ACROSS, W_DOWN, 1), (OUTWARD, W_DOWN, 0),
    (HEAD_PAIRS, 0, 2), (LEAVING, W_UP, 2), (HEAD_PAIRS, 0, 3), (LEAVING, W_UP, 3),
    (HEAD_PAIRS, 0, 4), (INWARD, W_GATE, 1), (HEAD_PAIRS, 0, 5), (ACROSS, W_GATE, 0),
    (STAYING, W_UP, 0), (REST, W_UP, 0), (OUTWARD, W_DOWN, 1), (HEAD_PAIRS, 0, 6),
    (STAYING, W_UP, 1), (REST, W_UP, 1), (HEAD_PAIRS, 0, 7), (INWARD, W_UP, 0), (ACROSS, W_GATE, 1),
    (STAYING, W_UP, 2), (LEAVING, W_OUT, 0), (REST, W_UP, 2), (STAYING, W_UP, 3), (REST, W_UP, 3),
    (LEAVING, W_OUT, 1), (OUTWARD, W_GATE, 0), (INWARD, W_UP, 1), (BLOCKS, W_V, 3),
    (BLOCKS, W_V, 2), (BLOCKS, W_V, 1), (STAYING, W_OUT, 0), (BLOCKS, W_V, 0), (REST, W_OUT, 0),
    (ACROSS, W_UP, 0), (BLOCKS, W_K, 3), (BLOCKS, W_K, 2), (INWARD, W_UP, 2), (STAYING, W_OUT, 1),
    (BLOCKS, W_K, 1), (REST, W_OUT, 1), (BLOCKS, W_K, 0), (LEAVING, W_V, 0), (ACROSS, W_UP, 1),
    (OUTWARD, W_GATE, 1), (BLOCKS, W_Q, 3), (LEAVING, W_V, 1), (INWARD, W_UP, 3), (BLOCKS, W_Q, 2),
    (BLOCKS, W_Q, 1), (BLOCKS, W_Q, 0), (QKV_TILES, 0, 0), (INWARD, W_OUT, 0), (ACROSS, W_UP, 2),
    (STAYING, W_V, 0), (REST, W_V, 0), (OUTWARD, W_UP, 0), (QKV_TILES, 0, 1), (INWARD, W_OUT, 1),
    (ACROSS, W_UP, 3), (LEAVING, W_K, 0), (STAYING, W_V, 1), (REST, W_V, 1), (OUTWARD, W_UP, 1),
    (QKV_TILES, 0, 2), (LEAVING, W_K, 1), (INWARD, W_V, 0), (ACROSS, W_OUT, 0), (QKV_TILES, 0, 3),
    (ACROSS, W_OUT, 1), (INWARD, W_V, 1), (STAYING, W_K, 0), (REST, W_K, 0), (OUTWARD, W_UP, 2),
    (NORM_ONE, 0, 0), (LEAVING, W_Q, 0), (ACROSS, W_V, 0), (LEAVING, W_Q, 1), (STAYING, W_K, 1),
    (REST, W_K, 1), (INWARD, W_K, 0), (ACROSS, W_V, 1), (OUTWARD, W_UP, 3), (OUTWARD, W_OUT, 0),
    (SMALL, 0, 1), (STAYING, W_Q, 0), (OUTWARD, W_OUT, 1), (REST, W_Q, 0), (SMALL, 0, 2),
    (STAYING, W_Q, 1), (INWARD, W_K, 1), (REST, W_Q, 1), (ACROSS, W_K, 0), (OUTWARD, W_V, 0),
    (SMALL, 0, 3), (INWARD, W_Q, 0), (OUTWARD, W_V, 1), (SMALL, 0, 4), (ACROSS, W_K, 1),
    (INWARD, W_Q, 1), (OUTWARD, W_K, 0), (SMALL, 0, 5), (ACROSS, W_Q, 0), (OUTWARD, W_K, 1),
    (ACROSS, W_Q, 1), (OUTWARD, W_Q, 0), (OUTWARD, W_Q, 1),
)


def backward_body(
    lay,
    lengths,
    in_cosine,
    in_sine,
    gains,
    sums,
    in_logs,
    full_qkv,
    full_out,
    full_gate,
    full_up,
    full_down,
    in_q,
    in_k,
    in_v,
    hidden_one2,
    attended2,
    hidden_two2,
    in_after,
    in_gate,
    in_up,
    in_product,
    in_grad_down,
    tokens,
    cotangent,
    output,
    grad_tokens,
    grad_first,
    sum_qkv,
    sum_out,
    sum_gate,
    sum_up,
    sum_down,
    small,
    cosine,
    sine,
    logs,
    gate,
    up,
    product,
    ring,
    w_out,
    one,
    two,
    three,
    cot,
    left,
    right,
    low,
    attend_grad,
    gate_sib,
    up_sib,
    low_sib,
    q_sib,
    k_sib,
    v_sib,
    held_down,
    held_gate,
    held_up,
    held_narrow,
    first_down,
    first_gate,
    first_up,
    first_narrow,
    later_down,
    later_gate,
    later_up,
    later_narrow,
    small_land,
    turned,
    load_sem,
    ring_sem,
    swap_send,
    swap_recv,
    write_sem,
    send,
    recv,
    z_send,
    z_recv,
    credit,
    f_local,
    f_send,
    f_recv,
    small_send,
    small_recv,
):
    place = Place(lay)
    line = Line(lay, place)
    count, c = place.count, place.c
    sibling = place.sibling()
    rows, width = cot.shape
    ff = gate.shape[1]
    side, narrow = ff // 2, width // 2
    block = min(TILE, rows)
    bits = place.bits

    barrier = pltpu.get_barrier_semaphore()
    partners = [place.partner(i) for i in range(bits)]
    known = [sibling] + partners + line.others + [line.next]
    for device in known:
        signal(barrier, device)

    @pl.when(line.inner)
    def _():
        signal(barrier, line.prev)
        pl.semaphore_wait(barrier, len(known) + 1)

    @pl.when(jnp.logical_not(line.inner))
    def _():
        pl.semaphore_wait(barrier, len(known))

    loads = {}

    def load(name, source, target):
        copy = pltpu.make_async_copy(source, target, load_sem.at[len(loads)])
        copy.start()
        loads[name] = copy

    writes = []

    def put(source, target):
        copy = pltpu.make_async_copy(source, target, write_sem.at[len(writes)])
        copy.start()
        writes.append(copy)
        return copy

    swaps = []

    def swap(source, target, begin=True):
        slot = len(swaps)
        copy = remote(source, target, swap_send.at[slot], swap_recv.at[slot], sibling)
        if begin:
            copy.start()
        swaps.append(copy)
        return copy

    def shard_of(p):
        m = sum(((p >> i) & 1) << (bits - 1 - i) for i in range(bits))
        return place.shard(m)

    sems = (send, recv, z_send, z_recv, credit, f_local, f_send, f_recv)
    half = count // 2
    down_rows = in_grad_down.shape[0] // count
    shard_rows = sum_qkv.shape[0]

    def down_block(p, window=None):
        at = pl.multiple_of(shard_of(p) * down_rows, down_rows)
        if window is None:
            return in_grad_down.at[pl.ds(at, down_rows), :]
        return in_grad_down.at[pl.ds(at + window.start, window.size), :]

    reduces = {}

    def reduce_of(name, held, first, later, final, offset, size):
        parts = BACKWARD_PARTS[name]
        part_rows = held.shape[1] // parts
        for part in range(parts):
            window = pl.ds(part * part_rows, part_rows)
            if name == W_DOWN:
                sources = [down_block(half + q, window) for q in range(half)]
            else:
                sources = [held.at[half + q, window] for q in range(half)]
            column = pl.ds(pl.multiple_of(offset + c * size, 128), size)
            reduces[name, part] = Reduce(
                place, line, len(reduces), window, held, sources, first, later, final, column, sems
            )

    def narrow_of(index, name, final, offset):
        at = index * count
        reduce_of(
            name,
            held_narrow.at[pl.ds(at, count)],
            first_narrow.at[pl.ds(index * half, half)],
            later_narrow.at[pl.ds(index * (half - 1), half - 1)],
            final,
            offset,
            narrow,
        )

    reduce_of(W_DOWN, held_down, first_down, later_down, sum_down, 0, narrow)
    reduce_of(W_GATE, held_gate, first_gate, later_gate, sum_gate, 0, side)
    reduce_of(W_UP, held_up, first_up, later_up, sum_up, 0, side)
    narrow_of(0, W_OUT, sum_out, 0)
    narrow_of(1, W_V, sum_qkv, 2 * width)
    narrow_of(2, W_K, sum_qkv, width)
    narrow_of(3, W_Q, sum_qkv, 0)

    def parts_of(name):
        return [reduces[name, i] for i in range(BACKWARD_PARTS[name])]

    smalls = []

    def small_step():
        slot = len(smalls)
        device = ([sibling] + partners + line.others)[slot]
        copy = remote(
            small_land.at[2 * slot],
            small_land.at[2 * slot + 1],
            small_send.at[slot],
            small_recv.at[slot],
            device,
        )
        small_land[2 * slot] = small[...]
        copy.start()
        smalls.append(copy)

    def small_take():
        smalls[-1].wait_recv()
        small[...] += small_land[2 * len(smalls) - 1]

    small_count = 1 + bits + len(line.others)

    def link(step):
        kind, who, part = step
        if kind == SMALL:
            while True:
                small_take()
                if len(smalls) == small_count:
                    return
                small_step()
                if part < 5:
                    return
        reduce = reduces[who, part]
        {
            LEAVING: reduce.leaving,
            STAYING: reduce.staying,
            REST: reduce.rest,
            INWARD: reduce.inward,
            ACROSS: reduce.across,
            OUTWARD: reduce.outward,
        }[kind]()

    for reduce in parts_of(W_DOWN):
        for q in reversed(range(half)):
            reduce.begin(q)

    tile = min(TILE, side)
    whole_tiles, rest = side // tile, side % tile

    def ring_copy(row, slot, size):
        return pltpu.make_async_copy(
            full_down.at[pl.ds(row, size), :],
            ring.at[slot, pl.ds(0, size), pl.ds(0, width)],
            ring_sem.at[slot],
        )

    theirs = pl.multiple_of((1 - c) * side, 128)
    ours = pl.multiple_of(c * side, 128)
    ring_copy(theirs, 0, tile).start()
    load("gate", in_gate, gate)
    load("up", in_up, up)
    load("cot", cotangent, cot)
    load("product", in_product, product)
    load("after", in_after, one)
    load("left", hidden_two2, left)
    down_loads = []
    for q in range(half):
        copy = pltpu.make_async_copy(down_block(q), held_down.at[q], load_sem.at[17 + q])
        copy.start()
        down_loads.append(copy)
    load("out", full_out, w_out)
    load("right", attended2, right)
    load("cosine", in_cosine, cosine)
    load("sine", in_sine, sine)
    load("logs", in_logs, logs)
    for name in ("gate", "up", "cot", "product", "after"):
        loads[name].wait()
    two[...] = one[...]

    def down_tile(at, slot, size):
        rows_of = ring[slot, 0:size, 0:width]
        grad_product = dot_nt(cot[...], rows_of)
        gate_pre = gate[:, pl.ds(at, size)].astype(F32)
        up_proj = up[:, pl.ds(at, size)].astype(F32)
        sigma = jax.nn.sigmoid(gate_pre)
        gate[:, pl.ds(at, size)] = (
            grad_product * up_proj * sigma * (1.0 + gate_pre * (1.0 - sigma))
        ).astype(BF16)
        up[:, pl.ds(at, size)] = (grad_product * (gate_pre * sigma)).astype(BF16)
        two[...] += dot_nn(product[:, pl.ds(at, size)], rows_of)

    gate_swap = swap(gate.at[:, pl.ds(theirs, side)], gate_sib, begin=False)
    up_swap = swap(up.at[:, pl.ds(theirs, side)], up_sib, begin=False)

    @pl.loop(0, 2)
    def _(turn):
        base = pl.multiple_of(lax.rem(1 - c + turn, 2) * side, 128)

        @pl.loop(0, whole_tiles)
        def _(t):
            slot = lax.rem(t, 2)
            at = pl.multiple_of(base + t * tile, 128)
            ring_copy(at, slot, tile).wait()

            @pl.when(t + 1 < whole_tiles)
            def _():
                ring_copy(pl.multiple_of(at + tile, 128), 1 - slot, tile).start()

            if rest:

                @pl.when(t + 1 == whole_tiles)
                def _():
                    ring_copy(pl.multiple_of(at + tile, 128), 2, rest).start()

            down_tile(at, slot, tile)

        @pl.when(turn == 0)
        def _():
            ring_copy(ours, 0, tile).start()

        if rest:
            at = pl.multiple_of(base + whole_tiles * tile, 128)
            ring_copy(at, 2, rest).wait()
            down_tile(at, 2, rest)

        @pl.when(turn == 0)
        def _():
            gate_swap.start()
            up_swap.start()

    low[...] = two[...].astype(BF16)
    output_put = put(low, output)
    load("q", in_q, product.at[:, pl.ds(0, width)])
    load("k", in_k, product.at[:, pl.ds(width, width)])

    def tile_copies(i):
        at = pl.ds(pl.multiple_of(i * block_w, block_w), block_w)
        slot = lax.rem(i, 2)
        return (
            pltpu.make_async_copy(
                full_gate.at[at, :], ring.at[slot, :, pl.ds(0, ff)], ring_sem.at[slot]
            ),
            pltpu.make_async_copy(
                full_up.at[at, :], ring.at[2 + slot, :, pl.ds(0, ff)], ring_sem.at[2 + slot]
            ),
        )

    block_w = min(TILE, width)
    start(tile_copies(0))
    start(tile_copies(1))

    def shard_at(p):
        flips = [place.flips[bits - 1 - i] * lax.rem(p // (1 << i), 2) for i in range(bits)]
        return place.f + sum(flips)

    def grad_blocks(who, both, own, other, links):
        parts = parts_of(who)
        held = parts[0].held

        @pl.loop(0, count)
        def _(i):
            p = count - 1 - i
            at = pl.ds(pl.multiple_of(shard_at(p) * shard_rows, 128), shard_rows)
            held[p] = (
                dot_tn(both[0:rows, at], own()) + dot_tn(both[rows : 2 * rows, at], other())
            ).astype(BF16)
            for q in range(half):

                @pl.when(p == half + q)
                def _():
                    for part in parts:
                        part.begin(q)

            between(i, links)

    def ours_of(ref, offset, size):
        at = pl.ds(pl.multiple_of(offset + c * size, 128), size)
        return lambda: ref[:, at]

    tiles = width // block_w

    def between(turn, links):
        for after, steps in enumerate(links):
            if steps:

                @pl.when(turn == after)
                def _():
                    for step in steps:
                        link(step)

    def back_tiles(links):
        @pl.loop(0, tiles)
        def _(i):
            wait(tile_copies(i))
            slot = lax.rem(i, 2)
            at = pl.ds(pl.multiple_of(i * block_w, block_w), block_w)
            two[:, at] = dot_nt(gate[...], ring[slot, :, 0:ff]) + dot_nt(
                up[...], ring[2 + slot, :, 0:ff]
            )

            @pl.when(i + 2 < tiles)
            def _():
                start(tile_copies(i + 2))

            between(i, links)

    def back_end():
        output_put.wait()
        small[...] = jnp.zeros(small.shape, F32)
        small[2:4, :] = sums[0:2, :]

        @pl.loop(0, rows // block)
        def _(i):
            at = pl.ds(pl.multiple_of(i * block, block), block)
            x = one[at, :]
            inverse = lax.rsqrt(jnp.mean(x * x, axis=-1, keepdims=True) + norm_eps)
            normed = x * inverse
            grad_hidden = two[at, :]
            small[1:2, :] += jnp.sum(grad_hidden * normed, axis=0, keepdims=True)
            result = cot[at, :].astype(F32) + rms_back(grad_hidden * gains[1:2, :], normed, inverse)
            three[at, :] = result
            low[at, :] = result.astype(BF16)

        low_swap.append(swap(low.at[:, pl.ds(theirs_narrow, narrow)], low_sib))
        gate_swap.wait_send()
        up_swap.wait_send()
        load("v", in_v, up.at[:, pl.ds(width, width)])
        load("tokens", tokens, cot)

    theirs_narrow = pl.multiple_of((1 - c) * narrow, 128)
    low_swap, head_swaps = [], {}

    def qkv_copy(i):
        at = pl.ds(pl.multiple_of(i * block_w, block_w), block_w)
        slot = lax.rem(i, 4)
        return pltpu.make_async_copy(full_qkv.at[at, :], ring.at[slot], ring_sem.at[slot])

    def attended_grad():
        loads["out"].wait()

        @pl.loop(0, rows // block)
        def _(i):
            at = pl.ds(pl.multiple_of(i * block, block), block)
            attend_grad[at, :] = dot_nt(low[at, :], w_out[...]).astype(BF16)

        for i in range(min(4, tiles)):
            qkv_copy(i).start()
        loads["right"].wait()
        low_swap[0].wait_recv()

    length = lengths[0]
    pairs = width // PAIR
    q_grad, k_grad = gate.at[:, pl.ds(0, width)], gate.at[:, pl.ds(width, width)]
    v_grad = up.at[:, pl.ds(0, width)]

    def attend_back(links):
        @pl.loop(0, pairs)
        def _(i):
            p = lax.rem((1 - c) * (pairs // 2) + i, pairs)
            at = pl.ds(pl.multiple_of(p * PAIR, PAIR), PAIR)
            shift = pl.ds(pl.multiple_of(width + p * PAIR, PAIR), PAIR)
            q, k, v, g = product[:, at], product[:, shift], up[:, shift], attend_grad[:, at]
            lane = lax.broadcasted_iota(jnp.int32, (rows, PAIR), 1)
            k_t = k.T
            sums_k, sums_v = [], []
            for head in range(2):
                inside = (lane // HEAD_DIM) == head
                k_head = jnp.where(inside, k, jnp.zeros_like(k))
                v_head = jnp.where(inside, v, jnp.zeros_like(v))
                k_turned = k_t[head * HEAD_DIM : (head + 1) * HEAD_DIM]
                parts_k, parts_v = [], []
                for b in range(rows // block):
                    upto = (b + 1) * block
                    q_block, g_block = q[b * block : upto], g[b * block : upto]
                    scores = dot_nt(k_head[:upto], q_block)
                    key = lax.broadcasted_iota(jnp.int32, scores.shape, 0)
                    query = lax.broadcasted_iota(jnp.int32, (1, block), 1) + b * block
                    log_total = logs[p, head : head + 1, b * block : upto]
                    allowed = key <= jnp.minimum(query, length - 1)
                    soft = jnp.where(allowed, jnp.exp(scores - log_total), 0.0)
                    grad_soft = dot_nt(v_head[:upto], g_block)
                    inner = jnp.sum(soft * grad_soft, axis=0, keepdims=True)
                    grad_scores = (soft * (grad_soft - inner)).astype(BF16)
                    turned[head * HEAD_DIM : (head + 1) * HEAD_DIM, b * block : upto] = dot_nn(
                        k_turned[:, :upto], grad_scores
                    )
                    parts_k.append(dot_nn(grad_scores, q_block))
                    parts_v.append(dot_nn(soft.astype(BF16), g_block))
                for parts, gathered in ((parts_k, sums_k), (parts_v, sums_v)):
                    rows_of = []
                    for r in range(rows // block):
                        piece = parts[r][r * block : (r + 1) * block]
                        for later in parts[r + 1 :]:
                            piece = piece + later[r * block : (r + 1) * block]
                        rows_of.append(piece)
                    gathered.append(jnp.concatenate(rows_of, axis=0))
            first_head = lane < HEAD_DIM
            cos, sin = cosine[...], sine[...]

            def back(x):
                return (x * cos - swap_halves(x) * sin).astype(BF16)

            gate[:, at] = back(turned[...].T * HEAD_DIM**-0.5)
            gate[:, shift] = back(jnp.where(first_head, sums_k[0], sums_k[1]))
            half_v = 0.5 * jnp.where(first_head, sums_v[0], sums_v[1])
            up[:, at] = half_v.astype(BF16)
            between(i, links)

            @pl.when(i == pairs // 2 - 1)
            def _():
                for copy in head_swaps.values():
                    copy.start()

    def qkv_tiles(links):
        @pl.loop(0, tiles)
        def _(i):
            qkv_copy(i).wait()
            slot = lax.rem(i, 4)
            at = pl.ds(pl.multiple_of(i * block_w, block_w), block_w)
            one[:, at] = (
                dot_nt(gate[:, 0:width], ring[slot, :, 0:width])
                + dot_nt(gate[:, width : 2 * width], ring[slot, :, width : 2 * width])
                + dot_nt(up[:, 0:width], ring[slot, :, 2 * width : 3 * width])
            )

            @pl.when(i + 4 < tiles)
            def _():
                qkv_copy(i + 4).start()

            between(i, links)

    def qkv_end():
        loads["tokens"].wait()
        low_swap[0].wait_send()

        @pl.loop(0, rows // block)
        def _(i):
            at = pl.ds(pl.multiple_of(i * block, block), block)
            x = cot[at, :].astype(F32)
            inverse = lax.rsqrt(jnp.mean(x * x, axis=-1, keepdims=True) + norm_eps)
            normed = x * inverse
            grad_hidden = one[at, :]
            small[0:1, :] += jnp.sum(grad_hidden * normed, axis=0, keepdims=True)
            grads = three[at, :] + rms_back(grad_hidden * gains[0:1, :], normed, inverse)
            low[at, :] = grads.astype(BF16)

        put(low, grad_tokens)
        small_step()

    def first_of(who):
        if who == W_GATE:
            loads["left"].wait()
            gate_swap.wait_recv()
        elif who == W_UP:
            up_swap.wait_recv()
        elif who in head_swaps:
            if who == W_V:
                loads["one"].wait()
            head_swaps[who].wait_recv()

    lefts = {
        W_GATE: (left, ours_of(gate, 0, side), lambda: gate_sib[...]),
        W_UP: (left, ours_of(up, 0, side), lambda: up_sib[...]),
        W_OUT: (right, ours_of(low, 0, narrow), lambda: low_sib[...]),
        W_V: (left, ours_of(up, 0, narrow), lambda: v_sib[...]),
        W_K: (left, ours_of(gate, width, narrow), lambda: k_sib[...]),
        W_Q: (left, ours_of(gate, 0, narrow), lambda: q_sib[...]),
    }

    def compute(kind):
        if kind == NORM_TWO:
            back_end()
        elif kind == ATTEND_GRAD:
            attended_grad()
        elif kind == NORM_ONE:
            qkv_end()

    def turns_of(kind, who, turns, every):
        links, at = [[] for _ in range(every)], 0
        while order and (order[0][0] <= SMALL or (order[0][0], order[0][1]) == (kind, who)):
            if order[0][0] == kind:
                order.pop(0)
                at += 1
            else:
                links[at].append(order.pop(0))
        spread = [[] for _ in range(turns)]
        for i, steps in enumerate(links):
            spread[(i + 1) * turns // every - 1] += steps
        return spread

    order = list(BACKWARD_ORDER)
    while order:
        step = order.pop(0)
        if step[0] <= SMALL:
            if step == (LEAVING, W_DOWN, 0):
                for copy in down_loads:
                    copy.wait()
            link(step)
        elif step[0] == HEAD_PAIRS:
            for key in ("q", "k", "v", "cosine", "sine", "logs"):
                loads[key].wait()
            for key, ref, land in ((W_V, v_grad, v_sib), (W_K, k_grad, k_sib), (W_Q, q_grad, q_sib)):
                head_swaps[key] = swap(ref.at[:, pl.ds(theirs_narrow, narrow)], land, begin=False)
            attend_back(turns_of(HEAD_PAIRS, 0, pairs, 8))
            put(v_grad, grad_first)
        elif step[0] == BLOCKS:
            who = step[1]
            first_of(who)
            grad_blocks(who, *lefts[who], turns_of(BLOCKS, who, count, 4))
            if who == W_UP:
                load("one", hidden_one2, left)
        elif step[0] == MLP_TILES:
            back_tiles(turns_of(MLP_TILES, 0, tiles, 4))
        elif step[0] == QKV_TILES:
            qkv_tiles(turns_of(QKV_TILES, 0, tiles, 4))
        else:
            compute(step[0])

    for reduce in reduces.values():
        reduce.drain()
    for copy in smalls:
        copy.wait_send()
    for copy in swaps:
        if not any(copy is item for item in (gate_swap, up_swap, low_swap[0])):
            copy.wait_send()
    for copy in writes:
        if copy is not output_put:
            copy.wait()


def backward_kernel(lay, lengths, tables, gains, sums, logs, weights, saved, tokens, cotangent):
    count = lay.fs
    half = count // 2
    rows, width = tokens.shape
    n, ff = weights[0].shape[1], weights[2].shape[1]
    shard, down = width // count, ff // count
    side, narrow = ff // 2, width // 2
    dma = pltpu.SemaphoreType.DMA
    vmem = pl.BlockSpec(memory_space=pltpu.VMEM)
    tall = pltpu.VMEM((rows, ff), BF16)
    flat = pltpu.VMEM((rows, width), BF16)
    full = pltpu.VMEM((rows, width), F32)
    small_steps = 1 + lay.bits + (lay.line.bit_length() - 1)
    parts = sum(BACKWARD_PARTS)
    operands = (lengths, *tables, gains, sums, logs, *weights, *saved, tokens, cotangent)
    return pl.pallas_call(
        functools.partial(backward_body, lay),
        in_specs=[pl.BlockSpec(memory_space=pltpu.SMEM)]
        + [ANY, ANY, vmem, vmem]
        + [ANY] * (len(operands) - 5),
        out_specs=[ANY] * 8 + [vmem],
        out_shape=[
            struct((rows, width), BF16),
            struct((rows, width), BF16),
            struct((rows, width), BF16),
            struct((shard, n), BF16),
            struct((shard, width), BF16),
            struct((shard, ff), BF16),
            struct((shard, ff), BF16),
            struct((down, width), BF16),
            struct((8, width), F32),
        ],
        scratch_shapes=[
            pltpu.VMEM((rows, PAIR), F32),
            pltpu.VMEM((rows, PAIR), F32),
            pltpu.VMEM(logs.shape, F32),
            tall,
            tall,
            tall,
            pltpu.VMEM((4, min(TILE, width), n), BF16),
            pltpu.VMEM((width, width), BF16),
            full,
            full,
            full,
            flat,
            pltpu.VMEM((2 * rows, width), BF16),
            pltpu.VMEM((2 * rows, width), BF16),
            flat,
            flat,
            pltpu.VMEM((rows, side), BF16),
            pltpu.VMEM((rows, side), BF16),
            pltpu.VMEM((rows, narrow), BF16),
            pltpu.VMEM((rows, narrow), BF16),
            pltpu.VMEM((rows, narrow), BF16),
            pltpu.VMEM((rows, narrow), BF16),
            pltpu.VMEM((half, down, narrow), BF16),
            pltpu.VMEM((count, shard, side), BF16),
            pltpu.VMEM((count, shard, side), BF16),
            pltpu.VMEM((4 * count, shard, narrow), BF16),
            pltpu.VMEM((half, down, narrow), BF16),
            pltpu.VMEM((half, shard, side), BF16),
            pltpu.VMEM((half, shard, side), BF16),
            pltpu.VMEM((4 * half, shard, narrow), BF16),
            pltpu.VMEM((half - 1, down, narrow), BF16),
            pltpu.VMEM((half - 1, shard, side), BF16),
            pltpu.VMEM((half - 1, shard, side), BF16),
            pltpu.VMEM((4 * (half - 1), shard, narrow), BF16),
            pltpu.VMEM((2 * small_steps, 8, width), F32),
            pltpu.VMEM((PAIR, rows), F32),
            dma((17 + half,)),
            dma((4,)),
            dma((6,)),
            dma((6,)),
            dma((3,)),
            dma((parts * count,)),
            dma((parts * count,)),
            dma((2 * parts,)),
            dma((2 * parts,)),
            pltpu.SemaphoreType.REGULAR((2 * parts,)),
            dma((parts,)),
            dma((parts,)),
            dma((parts,)),
            dma((small_steps,)),
            dma((small_steps,)),
        ],
        compiler_params=pltpu.CompilerParams(
            collective_id=1, has_side_effects=True, vmem_limit_bytes=63 * 2**20
        ),
        cost_estimate=pl.CostEstimate(
            flops=4 * rows * width * (n + width + 3 * ff),
            bytes_accessed=80 * 2**20,
            transcendentals=0,
        ),
        name="backward",
    )(*operands)


def finish_body(lay, entries, small, *refs):
    count = (len(refs) - 4) // 2
    sources, targets = refs[:count], refs[count : 2 * count]
    gain_one, gain_two, first_norm, value_norm = refs[2 * count :]
    for source, target in zip(sources, targets):
        target[...] = source[...].astype(target.dtype)

    @pl.when(pl.program_id(0) == 0)
    def _():
        rows = gain_one.shape[0]
        at = pl.ds(pl.multiple_of(lax.axis_index("fsdp") * rows, rows), rows)
        gain_one[...] = small[0, at]
        gain_two[...] = small[1, at]
        first_norm[0, 0] = jnp.sum(small[2:3, :]) / entries
        value_norm[0, 0] = jnp.sum(small[3:4, :]) / entries


def finish_kernel(lay, results):
    output, grad_tokens, grad_first, *totals, small = results
    rows, width = output.shape
    moved = [output, grad_tokens, grad_first, *totals]
    kinds = [BF16, F32, F32] + [F32] * len(totals)

    steps = 2

    def spec(item):
        return pl.BlockSpec((item.shape[0] // steps, item.shape[1]), lambda i: (i, 0))

    shard = width // lay.fs
    line = pl.BlockSpec((shard,), lambda i: (0,))
    scalar = pl.BlockSpec((1, 1), lambda i: (0, 0), memory_space=pltpu.SMEM)
    done = pl.pallas_call(
        functools.partial(finish_body, lay, rows * width * lay.dp * lay.fs),
        grid=(steps,),
        in_specs=[pl.BlockSpec(small.shape, lambda i: (0, 0))] + [spec(item) for item in moved],
        out_specs=[spec(item) for item in moved] + [line, line, scalar, scalar],
        out_shape=[struct(item.shape, kind) for item, kind in zip(moved, kinds)]
        + [struct((shard,), F32)] * 2
        + [struct((1, 1), F32)] * 2,
        compiler_params=pltpu.CompilerParams(vmem_limit_bytes=63 * 2**20),
        cost_estimate=pl.CostEstimate(
            flops=0, bytes_accessed=30 * 2**20, transcendentals=0
        ),
        name="finish",
    )(small, *moved)
    output, grad_tokens, grad_first, qkv, out, gate, up, down, gain_one, gain_two, first, value = done
    return (
        output,
        grad_tokens,
        grad_first,
        gain_one,
        qkv,
        out,
        gain_two,
        gate,
        up,
        down,
        first.reshape(()),
        value.reshape(()),
    )


def body(
    lay,
    tokens,
    first_values,
    lengths,
    gain_one,
    w_qkv,
    w_out,
    gain_two,
    w_gate,
    w_up,
    w_down,
    cotangent,
):
    rows, width = tokens.shape
    tables = tuple(jnp.asarray(table) for table in rotary_tables(rows))
    results = forward_kernel(
        lay, lengths, tokens, first_values, tables, gain_one, gain_two, cotangent, w_qkv, w_out, w_gate, w_up, w_down
    )
    weights, heads, logs, saved, gains, sums = (
        results[:5],
        results[5:8],
        results[8],
        results[9:17],
        results[17],
        results[18],
    )
    results = backward_kernel(
        lay, lengths, tables, gains, sums, logs, weights, (*heads, *saved), tokens, cotangent
    )
    return finish_kernel(lay, results)


def solution(mesh):
    both = P(AXES, None)
    rows = P("fsdp", None)
    in_specs = (both, both, P(AXES), P("fsdp"), rows, rows, P("fsdp"), rows, rows, rows, both)
    out_specs = (both, both, both, P("fsdp"), rows, rows, P("fsdp"), rows, rows, rows, P(), P())
    lay = Layout(mesh.shape["dp"], mesh.shape["fsdp"])
    return jax.shard_map(
        functools.partial(body, lay),
        mesh=mesh,
        in_specs=in_specs,
        out_specs=out_specs,
        check_vma=False,
    )
```

profile of v0, /device:TPU:0, one launch (start us, length us, event | category | flops | bytes accessed | tf_op | source)
XLA Modules:
  0.0 238.8 jit_solution(10232505986159864299)
XLA Ops:
  1.3 92.5 %forward.1 = (bf16[1024,3072]{1,0:T(8,128)(2,1)}, bf16[1024,1024]{1,0:T(8,128)(2,1)}, bf16[1024,2816]{1,0:T(8,128)(2,1)}, bf16[1024,2816]{1,0:T(8,128)(2,1)}, bf...) custom-call(s32[1]{0:T(128)S(6)} %copy.25.lengths, ...), custom_call_target="tpu_custom_call" | custom-call | flops 13153337344 | bytes 62914560 | tf_op jit(solution)/shard_map/forward/pallas_call | solution.py:639
  93.8 134.9 %backward.1 = (bf16[512,1024]{1,0:T(8,128)(2,1)}, bf16[512,1024]{1,0:T(8,128)(2,1)}, bf16[512,1024]{1,0:T(8,128)(2,1)}, bf16[256,3072]{1,0:T(8,128)(2,1)}, bf16[...) custom-call(s32[1]{0:T(128)S(6)} %copy.25.lengths, ...), custom_call_target="tpu_custom_call" | custom-call | flops 26306674688 | bytes 83886080 | tf_op jit(solution)/shard_map/backward/pallas_call | solution.py:1549
  228.7 9.9 %finish.1 = (bf16[512,1024]{1,0:T(8,128)(2,1)}, f32[512,1024]{1,0:T(8,128)}, f32[512,1024]{1,0:T(8,128)}, f32[256,3072]{1,0:T(8,128)}, f32[256,1024]{1,0:T(8,128...) custom-call(f32[8,1024]{1,0:T(8,128)} %get-tuple-element.71.small, ...), custom_call_target="tpu_custom_call" | custom-call | bytes 31457280 | tf_op jit(solution)/shard_map/finish/pallas_call | solution.py:1662
where the time goes:
time: 239 us
  Pallas kernels  237 us (99%)
    pallas_call x1, Pallas kernels, backward_kernel(): pl.pallas_call(functools.partial(backward_body, lay), in_specs=[pl.BlockS...  135 us
    pallas_call x1, Pallas kernels, forward_kernel(): pl.pallas_call(functools.partial(forward_body, lay), in_specs=[pl.BlockSp...  92.5 us
    pallas_call x1, Pallas kernels, finish_kernel(): pl.pallas_call(functools.partial(finish_body, lay, rows * width * lay.dp...  9.92 us

commit v1 on v0

--- a/solution.py
+++ b/solution.py
@@ -187,18 +187,18 @@
 NORMALISE, QUERIES, KEYS, VALUES, HEADS, PROJECT, GATES, UPS, SUM_DOWN = range(4, 13)
 FORWARD_LIFTED = (QK, V, GATE, DOWN)
 FORWARD_ORDER = (
-    (BEGIN, QK, 1), (BEGIN, QK, 2), (BEGIN, V, 1), (BEGIN, V, 2), (BEGIN, GATE, 1),
-    (NORMALISE, 0, 0), (ARRIVE, QK, 1), (ARRIVE, QK, 2), (LIFT, QK, 1), (LIFT, QK, 2),
-    (ARRIVE, V, 1), (BEGIN, GATE, 2), (ARRIVE, V, 2), (ARRIVE, GATE, 1), (BEGIN, OUT, 1),
-    (ARRIVE, QK, 3), (LIFT, QK, 3), (LAND, QK, 1), (LIFT, V, 1), (BEGIN, UP, 1), (ARRIVE, V, 3),
-    (BEGIN, OUT, 2), (LIFT, V, 2), (LAND, QK, 2), (ARRIVE, OUT, 1), (BEGIN, DOWN, 1), (LIFT, V, 3),
-    (LAND, QK, 3), (QUERIES, 0, 0), (ARRIVE, GATE, 2), (LAND, V, 1), (KEYS, 0, 0), (LIFT, GATE, 1),
-    (LAND, V, 2), (LIFT, GATE, 2), (ARRIVE, OUT, 2), (LAND, V, 3), (VALUES, 0, 0), (BEGIN, UP, 2),
-    (HEADS, 0, 0), (ARRIVE, UP, 1), (ARRIVE, GATE, 3), (HEADS, 0, 0), (LAND, GATE, 1),
-    (LIFT, GATE, 3), (ARRIVE, OUT, 3), (BEGIN, DOWN, 2), (HEADS, 0, 0), (ARRIVE, DOWN, 1),
-    (LAND, GATE, 2), (HEADS, 0, 0), (LIFT, DOWN, 1), (PROJECT, 0, 0), (LAND, GATE, 3),
-    (ARRIVE, UP, 2), (GATES, 0, 0), (ARRIVE, UP, 3), (ARRIVE, DOWN, 2), (LIFT, DOWN, 2),
-    (UPS, 0, 0), (ARRIVE, DOWN, 3), (LIFT, DOWN, 3), (LAND, DOWN, 1), (UPS, 0, 1), (LAND, DOWN, 2),
+    (BEGIN, QK, 1), (BEGIN, QK, 2), (NORMALISE, 0, 0), (BEGIN, GATE, 1), (ARRIVE, QK, 1),
+    (ARRIVE, QK, 2), (LIFT, QK, 2), (BEGIN, V, 1), (LIFT, QK, 1), (BEGIN, OUT, 1), (BEGIN, V, 2),
+    (ARRIVE, V, 1), (BEGIN, GATE, 2), (ARRIVE, V, 2), (ARRIVE, GATE, 1), (ARRIVE, QK, 3),
+    (LIFT, QK, 3), (LAND, QK, 2), (ARRIVE, V, 3), (ARRIVE, OUT, 1), (BEGIN, OUT, 2), (LIFT, V, 2),
+    (ARRIVE, GATE, 2), (LAND, QK, 1), (BEGIN, UP, 1), (LIFT, V, 1), (LAND, QK, 3), (LIFT, V, 3),
+    (QUERIES, 0, 0), (LAND, V, 2), (LIFT, GATE, 1), (ARRIVE, GATE, 3), (BEGIN, DOWN, 1),
+    (BEGIN, UP, 2), (LIFT, GATE, 2), (BEGIN, DOWN, 2), (KEYS, 0, 0), (LAND, V, 1), (LAND, V, 3),
+    (VALUES, 0, 0), (ARRIVE, OUT, 3), (LIFT, GATE, 3), (HEADS, 0, 0), (HEADS, 0, 0),
+    (LAND, GATE, 1), (ARRIVE, OUT, 2), (HEADS, 0, 0), (ARRIVE, UP, 1), (HEADS, 0, 0),
+    (ARRIVE, DOWN, 1), (ARRIVE, UP, 2), (LAND, GATE, 2), (LIFT, DOWN, 1), (PROJECT, 0, 0),
+    (ARRIVE, DOWN, 2), (LIFT, DOWN, 2), (LAND, GATE, 3), (GATES, 0, 0), (ARRIVE, UP, 3),
+    (LAND, DOWN, 1), (UPS, 0, 0), (ARRIVE, DOWN, 3), (LIFT, DOWN, 3), (UPS, 0, 1), (LAND, DOWN, 2),
     (SUM_DOWN, 0, 0), (LAND, DOWN, 3),
 )
 
@@ -871,7 +871,7 @@
 
 
 W_DOWN, W_GATE, W_UP, W_OUT, W_V, W_K, W_Q = range(7)
-BACKWARD_PARTS = (2, 2, 4, 2, 2, 2, 2)
+BACKWARD_PARTS = (2, 2, 4, 2, 2, 4, 4)
 LEAVING, STAYING, REST, INWARD, ACROSS, OUTWARD, SMALL = range(7)
 BLOCKS, MLP_TILES, NORM_TWO, ATTEND_GRAD, HEAD_PAIRS, QKV_TILES, NORM_ONE = range(7, 14)
 BACKWARD_ORDER = (
@@ -896,17 +896,22 @@
     (BLOCKS, W_K, 1), (REST, W_OUT, 1), (BLOCKS, W_K, 0), (LEAVING, W_V, 0), (ACROSS, W_UP, 1),
     (OUTWARD, W_GATE, 1), (BLOCKS, W_Q, 3), (LEAVING, W_V, 1), (INWARD, W_UP, 3), (BLOCKS, W_Q, 2),
     (BLOCKS, W_Q, 1), (BLOCKS, W_Q, 0), (QKV_TILES, 0, 0), (INWARD, W_OUT, 0), (ACROSS, W_UP, 2),
-    (STAYING, W_V, 0), (REST, W_V, 0), (OUTWARD, W_UP, 0), (QKV_TILES, 0, 1), (INWARD, W_OUT, 1),
-    (ACROSS, W_UP, 3), (LEAVING, W_K, 0), (STAYING, W_V, 1), (REST, W_V, 1), (OUTWARD, W_UP, 1),
-    (QKV_TILES, 0, 2), (LEAVING, W_K, 1), (INWARD, W_V, 0), (ACROSS, W_OUT, 0), (QKV_TILES, 0, 3),
-    (ACROSS, W_OUT, 1), (INWARD, W_V, 1), (STAYING, W_K, 0), (REST, W_K, 0), (OUTWARD, W_UP, 2),
-    (NORM_ONE, 0, 0), (LEAVING, W_Q, 0), (ACROSS, W_V, 0), (LEAVING, W_Q, 1), (STAYING, W_K, 1),
-    (REST, W_K, 1), (INWARD, W_K, 0), (ACROSS, W_V, 1), (OUTWARD, W_UP, 3), (OUTWARD, W_OUT, 0),
-    (SMALL, 0, 1), (STAYING, W_Q, 0), (OUTWARD, W_OUT, 1), (REST, W_Q, 0), (SMALL, 0, 2),
-    (STAYING, W_Q, 1), (INWARD, W_K, 1), (REST, W_Q, 1), (ACROSS, W_K, 0), (OUTWARD, W_V, 0),
-    (SMALL, 0, 3), (INWARD, W_Q, 0), (OUTWARD, W_V, 1), (SMALL, 0, 4), (ACROSS, W_K, 1),
-    (INWARD, W_Q, 1), (OUTWARD, W_K, 0), (SMALL, 0, 5), (ACROSS, W_Q, 0), (OUTWARD, W_K, 1),
-    (ACROSS, W_Q, 1), (OUTWARD, W_Q, 0), (OUTWARD, W_Q, 1),
+    (STAYING, W_V, 0), (REST, W_V, 0), (OUTWARD, W_UP, 0), (QKV_TILES, 0, 1), (LEAVING, W_K, 0),
+    (INWARD, W_OUT, 1), (LEAVING, W_K, 1), (ACROSS, W_UP, 3), (LEAVING, W_K, 2), (STAYING, W_V, 1),
+    (REST, W_V, 1), (LEAVING, W_K, 3), (INWARD, W_V, 0), (ACROSS, W_OUT, 0), (OUTWARD, W_UP, 1),
+    (QKV_TILES, 0, 2), (STAYING, W_K, 0), (REST, W_K, 0), (ACROSS, W_OUT, 1), (STAYING, W_K, 1),
+    (REST, W_K, 1), (OUTWARD, W_UP, 2), (QKV_TILES, 0, 3), (INWARD, W_V, 1), (INWARD, W_K, 0),
+    (LEAVING, W_Q, 0), (ACROSS, W_V, 0), (LEAVING, W_Q, 1), (STAYING, W_K, 2), (REST, W_K, 2),
+    (LEAVING, W_Q, 2), (INWARD, W_K, 1), (STAYING, W_K, 3), (REST, W_K, 3), (LEAVING, W_Q, 3),
+    (OUTWARD, W_UP, 3), (OUTWARD, W_OUT, 0), (NORM_ONE, 0, 0), (INWARD, W_K, 2), (INWARD, W_K, 3),
+    (ACROSS, W_V, 1), (ACROSS, W_K, 0), (ACROSS, W_K, 1), (STAYING, W_Q, 0), (REST, W_Q, 0),
+    (STAYING, W_Q, 1), (REST, W_Q, 1), (SMALL, 0, 1), (STAYING, W_Q, 2), (REST, W_Q, 2),
+    (ACROSS, W_K, 2), (STAYING, W_Q, 3), (REST, W_Q, 3), (OUTWARD, W_OUT, 1), (OUTWARD, W_V, 0),
+    (ACROSS, W_K, 3), (INWARD, W_Q, 0), (OUTWARD, W_V, 1), (SMALL, 0, 2), (INWARD, W_Q, 1),
+    (OUTWARD, W_K, 0), (INWARD, W_Q, 2), (SMALL, 0, 3), (ACROSS, W_Q, 0), (OUTWARD, W_K, 1),
+    (INWARD, W_Q, 3), (OUTWARD, W_K, 2), (ACROSS, W_Q, 1), (SMALL, 0, 4), (OUTWARD, W_K, 3),
+    (ACROSS, W_Q, 2), (OUTWARD, W_Q, 0), (ACROSS, W_Q, 3), (SMALL, 0, 5), (OUTWARD, W_Q, 1),
+    (OUTWARD, W_Q, 2), (OUTWARD, W_Q, 3),
 )
 
 

time: 239 us -> 236 us (0.987)
  Pallas kernels: 237 us -> 234 us
    pallas_call x1, Pallas kernels: 92.5 us -> 89.7 us  [forward_kernel(): pl.pallas_call(functools.partial(forward_body, lay), in_specs=[pl.BlockSp...]
where the time goes in v1:
time: 236 us
  Pallas kernels  234 us (99%)
    pallas_call x1, Pallas kernels, backward_kernel(): pl.pallas_call(functools.partial(backward_body, lay), in_specs=[pl.BlockS...  135 us
    pallas_call x1, Pallas kernels, forward_kernel(): pl.pallas_call(functools.partial(forward_body, lay), in_specs=[pl.BlockSp...  89.7 us
    pallas_call x1, Pallas kernels, finish_kernel(): pl.pallas_call(functools.partial(finish_body, lay, rows * width * lay.dp...  9.92 us

profile of v1, /device:TPU:0, one launch (start us, length us, event | category | flops | bytes accessed | tf_op | source)
XLA Modules:
  0.0 235.8 jit_solution(2113458350547281676)
XLA Ops:
  1.3 89.7 %forward.1 = (bf16[1024,3072]{1,0:T(8,128)(2,1)}, bf16[1024,1024]{1,0:T(8,128)(2,1)}, bf16[1024,2816]{1,0:T(8,128)(2,1)}, bf16[1024,2816]{1,0:T(8,128)(2,1)}, bf...) custom-call(s32[1]{0:T(128)S(6)} %copy.25.lengths, ...), custom_call_target="tpu_custom_call" | custom-call | flops 13153337344 | bytes 62914560 | tf_op jit(solution)/shard_map/forward/pallas_call | solution.py:639
  91.0 134.7 %backward.1 = (bf16[512,1024]{1,0:T(8,128)(2,1)}, bf16[512,1024]{1,0:T(8,128)(2,1)}, bf16[512,1024]{1,0:T(8,128)(2,1)}, bf16[256,3072]{1,0:T(8,128)(2,1)}, bf16[...) custom-call(s32[1]{0:T(128)S(6)} %copy.25.lengths, ...), custom_call_target="tpu_custom_call" | custom-call | flops 26306674688 | bytes 83886080 | tf_op jit(solution)/shard_map/backward/pallas_call | solution.py:1554
  225.7 9.9 %finish.1 = (bf16[512,1024]{1,0:T(8,128)(2,1)}, f32[512,1024]{1,0:T(8,128)}, f32[512,1024]{1,0:T(8,128)}, f32[256,3072]{1,0:T(8,128)}, f32[256,1024]{1,0:T(8,128...) custom-call(f32[8,1024]{1,0:T(8,128)} %get-tuple-element.71.small, ...), custom_call_target="tpu_custom_call" | custom-call | bytes 31457280 | tf_op jit(solution)/shard_map/finish/pallas_call | solution.py:1667

commit v2 on v1

--- a/solution.py
+++ b/solution.py
@@ -253,7 +253,7 @@
     values,
     attended,
     after,
-    gate_pre,
+    activated,
     low_gate,
     low_up,
     product2,
@@ -487,13 +487,13 @@
         low_up[at, 0:width] = (x * scale * gains[1:2, :]).astype(BF16)
 
     def gate_rows(at):
-        gate_pre[at, :] = dot_nn(low_up[at, 0:width], w_gate[...])
-        low_gate[at, :] = gate_pre[at, :].astype(BF16)
+        raw = dot_nn(low_up[at, 0:width], w_gate[...])
+        low_gate[at, :] = raw.astype(BF16)
+        activated[at, :] = raw * jax.nn.sigmoid(raw)
 
     def up_rows(at):
         up_proj = dot_nn(low_up[at, 0:width], w_up[...])
-        gate_of = gate_pre[at, :]
-        product2[at, :] = (gate_of * jax.nn.sigmoid(gate_of) * up_proj).astype(BF16)
+        product2[at, :] = (activated[at, :] * up_proj).astype(BF16)
         low_up[at, :] = up_proj.astype(BF16)
 
     def compute(kind, part):
@@ -548,12 +548,16 @@
             for copy in product_swaps:
                 copy.wait_recv()
 
-            @pl.loop(0, ff // TILE)
-            def _(i):
-                at = pl.ds(pl.multiple_of(i * TILE, TILE), TILE)
-                grad_low[at, :] = dot_tn(product2[:, at], cot2[...]).astype(BF16)
-
-            put(grad_low, grad_down)
+            size = ff // TILE // 2 * TILE
+            for first_row, last_row in ((0, size), (size, ff)):
+
+                @pl.loop(first_row // TILE, last_row // TILE)
+                def _(i):
+                    at = pl.ds(pl.multiple_of(i * TILE, TILE), TILE)
+                    grad_low[at, :] = dot_tn(product2[:, at], cot2[...]).astype(BF16)
+
+                part = pl.ds(first_row, last_row - first_row)
+                put(grad_low.at[part, :], grad_down.at[part, :])
 
     def up_parts(steps):
         size = rows // 2
@@ -671,7 +675,7 @@
             dma((count - 1,)),
             dma((6,)),
             dma((6,)),
-            dma((16,)),
+            dma((18,)),
         ],
         compiler_params=pltpu.CompilerParams(
             collective_id=0, has_side_effects=True, vmem_limit_bytes=62 * 2**20

time: 236 us -> 236 us (level)
  no operation moved by 1% of the time
where the time goes in v2:
time: 236 us
  Pallas kernels  234 us (99%)
    pallas_call x1, Pallas kernels, backward_kernel(): pl.pallas_call(functools.partial(backward_body, lay), in_specs=[pl.BlockS...  135 us
    pallas_call x1, Pallas kernels, forward_kernel(): pl.pallas_call(functools.partial(forward_body, lay), in_specs=[pl.BlockSp...  89.6 us
    pallas_call x1, Pallas kernels, finish_kernel(): pl.pallas_call(functools.partial(finish_body, lay, rows * width * lay.dp...  9.92 us

profile of v2, /device:TPU:0, one launch (start us, length us, event | category | flops | bytes accessed | tf_op | source)
XLA Modules:
  0.0 235.8 jit_solution(11999141780398420116)
XLA Ops:
  1.3 89.6 %forward.1 = (bf16[1024,3072]{1,0:T(8,128)(2,1)}, bf16[1024,1024]{1,0:T(8,128)(2,1)}, bf16[1024,2816]{1,0:T(8,128)(2,1)}, bf16[1024,2816]{1,0:T(8,128)(2,1)}, bf...) custom-call(s32[1]{0:T(128)S(6)} %copy.25.lengths, ...), custom_call_target="tpu_custom_call" | custom-call | flops 13153337344 | bytes 62914560 | tf_op jit(solution)/shard_map/forward/pallas_call | solution.py:643
  90.9 134.7 %backward.1 = (bf16[512,1024]{1,0:T(8,128)(2,1)}, bf16[512,1024]{1,0:T(8,128)(2,1)}, bf16[512,1024]{1,0:T(8,128)(2,1)}, bf16[256,3072]{1,0:T(8,128)(2,1)}, bf16[...) custom-call(s32[1]{0:T(128)S(6)} %copy.25.lengths, ...), custom_call_target="tpu_custom_call" | custom-call | flops 26306674688 | bytes 83886080 | tf_op jit(solution)/shard_map/backward/pallas_call | solution.py:1558
  225.7 9.9 %finish.1 = (bf16[512,1024]{1,0:T(8,128)(2,1)}, f32[512,1024]{1,0:T(8,128)}, f32[512,1024]{1,0:T(8,128)}, f32[256,3072]{1,0:T(8,128)}, f32[256,1024]{1,0:T(8,128...) custom-call(f32[8,1024]{1,0:T(8,128)} %get-tuple-element.71.small, ...), custom_call_target="tpu_custom_call" | custom-call | bytes 31457280 | tf_op jit(solution)/shard_map/finish/pallas_call | solution.py:1671
